TPU v7x, 32 devices: a whole 2x2x4 slice. The times are simulated.
32 devices in a mesh: depth: 4 (over x, core), row: 4 (over z), col: 2 (over y).
Axes of the slice: x: 2, y: 2, z: 4, core: 2. Of those that a mesh axis runs over, the one named last changes fastest.
Arguments:
- density: float32 [4096, 4096], P('row', ('depth', 'col')), as said below
- pattern: int32 [64, 64], replicated, may hold values from 0 to 1, as said below
- filters: int32 [4, 64, 64], replicated, may hold values from 0 to 1, as said below
Outputs:
- purified: float32 [4096, 4096], P('row', ('depth', 'col'))
Inputs may be any that keep to these rules, and one draw needn't show every extreme that they name: density is symmetric. `pattern`: symmetric 0/1 block table with every diagonal block set. `filters`: each table is a symmetric 0/1 block table with every diagonal block set.
All inputs are finite; a program needn't handle non-finite values.
Results may differ from a plain program's by a relative error of at most 0.007.
Values may be sent and summed in bfloat16 or wider, within the bound.
A program may use at most 64 MiB of HBM per device.

v0:
```python
import functools

import jax
import jax.numpy as jnp
from jax import lax
from jax.experimental import pallas as pl
from jax.experimental.pallas import tpu as pltpu
from jax.sharding import PartitionSpec as P

BLK = 64
PURIFY = 2
CORES = 2
LANES = 128
MESH = pl.DeviceIdType.MESH


def kernel(dims, dens, tabs, out, a_row, a_col, s_row, sq, acc, mask,
           z_send, z_recv, a_send, a_recv, af_send, af_recv,
           s_send, s_recv, sf_send, sf_recv):
    nd, nr, nc, h, w, tm, cuts = dims
    Q = len(cuts)
    G = w // LANES
    nx = nd // CORES
    m = h // w
    rb, sb = h // BLK, w // BLK
    d, r, c = lax.axis_index("depth"), lax.axis_index("row"), lax.axis_index("col")
    x, core = d // CORES, d % CORES
    sib = x * CORES + (1 - core)
    me = d * nc + c
    peers = [(px, pc) for px in range(nx) for pc in range(nc) if px or pc]
    direct = [p for p, (px, pc) in enumerate(peers) if not (px and pc)]
    bent = [p for p, (px, pc) in enumerate(peers) if px and pc]

    def dev(dd, rr, cc):
        return (dd, rr, cc)

    def peer_to(p):
        px, pc = peers[p]
        return ((x + px) % nx) * CORES + core, (c + pc) % nc

    def peer_from(p, k):
        px, pc = peers[p]
        return ((x + nx - px) % nx) * CORES + k, (c + nc - pc) % nc

    bar = pltpu.get_barrier_semaphore()
    for p in direct:
        dd, cc = peer_to(p)
        pl.semaphore_signal(bar, inc=1, device_id=dev(dd, r, cc), device_id_type=MESH)
    pl.semaphore_signal(bar, inc=1, device_id=dev(sib, r, c), device_id_type=MESH)

    @pl.when(r > 0)
    def _():
        pl.semaphore_signal(bar, inc=1, device_id=dev(d, r - 1, c), device_id_type=MESH)

    @pl.when(r < nr - 1)
    def _():
        pl.semaphore_signal(bar, inc=1, device_id=dev(d, r + 1, c), device_id_type=MESH)

    tb = tm // BLK
    slot = lax.broadcasted_iota(jnp.int32, (h // tm * 8, tabs.shape[1]), 0)
    r_pick = (slot // 8 * tb + slot % 8 + r * rb
              == lax.broadcasted_iota(jnp.int32, (h // tm * 8, tabs.shape[1]), 1)).astype(jnp.float32)
    c_pick = ((lax.broadcasted_iota(jnp.int32, (tabs.shape[2], w), 1) // BLK + me * sb)
              == lax.broadcasted_iota(jnp.int32, (tabs.shape[2], w), 0)).astype(jnp.float32)
    for k in range(tabs.shape[0]):
        rows = jnp.dot(r_pick, tabs[k].astype(jnp.float32), preferred_element_type=jnp.float32)
        mask[k] = jnp.dot(rows, c_pick, preferred_element_type=jnp.float32)

    def tile_mask(k, t, g0, g1):
        n = (g1 - g0) * LANES
        mk = mask[k, pl.ds(pl.multiple_of(t * 8, 8), 8), g0 * LANES:g1 * LANES][:tb]
        return jnp.broadcast_to(mk[:, None, :], (tb, BLK, n)).reshape(tm, n)

    def rows_of(t):
        return pl.ds(pl.multiple_of(t * tm, tm), tm)

    @pl.loop(0, h // tm)
    def _(t):
        for g in range(G):
            v = (dens[rows_of(t), g * LANES:(g + 1) * LANES] * tile_mask(0, t, g, g + 1)).astype(jnp.bfloat16)
            a_col[0, r, g, rows_of(t), :] = v
            a_row[0, me, g, rows_of(t), :] = v

    near = jnp.minimum(r, 1) + jnp.minimum(nr - 1 - r, 1)
    for n in range(3):
        @pl.when(near == n)
        def _():
            pl.semaphore_wait(bar, len(direct) + 1 + n)

    def z_copy(s, q, src, up):
        ref = a_col.at[s, src, cuts[q][0]:cuts[q][1]]
        return pltpu.make_async_remote_copy(
            src_ref=ref, dst_ref=ref, send_sem=z_send.at[s, q, src, up],
            recv_sem=z_recv.at[s, q, src],
            device_id=dev(d, r + 1 if up else r - 1, c), device_id_type=MESH)

    def z_own(s, q, op):
        @pl.when(r < nr - 1)
        def _():
            getattr(z_copy(s, q, r, 1), op)()

        @pl.when(r > 0)
        def _():
            getattr(z_copy(s, q, r, 0), op)()

    def z_arrive(s, q, dist):
        @pl.when(r + dist < nr)
        def _():
            z_copy(s, q, r + dist, 1).wait_recv()

            @pl.when(r > 0)
            def _():
                z_copy(s, q, r + dist, 0).start()

        @pl.when(r - dist >= 0)
        def _():
            z_copy(s, q, r - dist, 0).wait_recv()

            @pl.when(r < nr - 1)
            def _():
                z_copy(s, q, r - dist, 1).start()

    def z_drain(s, q):
        z_own(s, q, "wait_send")
        for dist in range(1, nr - 1):
            @pl.when((r + dist < nr) & (r > 0))
            def _():
                z_copy(s, q, r + dist, 0).wait_send()

            @pl.when((r - dist >= 0) & (r < nr - 1))
            def _():
                z_copy(s, q, r - dist, 1).wait_send()

    def ac(ref, ss, rs, to):
        return pltpu.make_async_remote_copy(
            src_ref=ref, dst_ref=ref, send_sem=ss, recv_sem=rs,
            device_id=dev(to[0], r, to[1]), device_id_type=MESH)

    class Gather:
        def __init__(self, view, send, recv, fsend, frecv):
            self.view, self.send, self.recv = view, send, recv
            self.fsend, self.frecv = fsend, frecv

        def block(self, p, k):
            dd, cc = peer_from(p, k)
            return self.view(dd * nc + cc)

        def half(self, dd, cc, i):
            return self.view(dd * nc + cc).at[:, i * (h // 2):(i + 1) * (h // 2), :]

        def own(self, p):
            return ac(self.view(me), self.send(p, 0), self.recv(p, 0), peer_to(p))

        def got(self, p, i=None):
            if i is None:
                return ac(self.block(p, core), self.send(p, 0), self.recv(p, 0), peer_to(p))
            dd, cc = peer_from(p, core)
            return ac(self.half(dd, cc, i), self.send(p, i), self.recv(p, i), peer_to(p))

        def turn(self, p, i):
            px, pc = peers[p]
            if i == 0:
                ref = self.half(((x + nx - px) % nx) * CORES + core, c, 0)
                to = (d, (c + pc) % nc)
            else:
                ref = self.half(d, (c + nc - pc) % nc, 1)
                to = (((x + px) % nx) * CORES + core, c)
            return ac(ref, self.send(p, i), self.recv(p, i), to)

        def fwd(self, p):
            ref = self.view(me) if p == len(peers) else self.block(p, core)
            return ac(ref, self.fsend(p), self.frecv(p), (sib, c))

        def fgot(self, p):
            ref = self.view(sib * nc + c) if p == len(peers) else self.block(p, 1 - core)
            return ac(ref, self.fsend(p), self.frecv(p), (sib, c))

        def begin(self):
            for p in direct:
                self.own(p).start()
            self.fwd(len(peers)).start()

        def hop(self):
            for q in direct:
                self.got(q).wait_recv()
                for p in bent:
                    if peers[q] == (peers[p][0], 0):
                        self.turn(p, 0).start()
                    if peers[q] == (0, peers[p][1]):
                        self.turn(p, 1).start()
            for q in direct:
                self.fwd(q).start()

        def relay(self):
            for p in bent:
                self.got(p, 0).wait_recv()
                self.got(p, 1).wait_recv()
                self.fwd(p).start()

        def finish(self):
            for p in range(len(peers) + 1):
                self.fgot(p).wait_recv()

        def drain(self):
            for p in direct:
                self.own(p).wait_send()
            for p in bent:
                self.turn(p, 0).wait_send()
                self.turn(p, 1).wait_send()
            for p in range(len(peers) + 1):
                self.fwd(p).wait_send()

    ga = [Gather(lambda j, s=s: a_row.at[s, j], lambda p, i, s=s: a_send.at[s, p, i],
                 lambda p, i, s=s: a_recv.at[s, p, i], lambda p, s=s: af_send.at[s, p],
                 lambda p, s=s: af_recv.at[s, p]) for s in range(PURIFY)]
    gs = [[Gather(lambda j, s=s, q=q: s_row.at[s, j, cuts[q][0]:cuts[q][1]],
                  lambda p, i, s=s, q=q: s_send.at[s, q, p, i],
                  lambda p, i, s=s, q=q: s_recv.at[s, q, p, i],
                  lambda p, s=s, q=q: sf_send.at[s, q, p],
                  lambda p, s=s, q=q: sf_recv.at[s, q, p]) for q in range(Q)] for s in range(PURIFY)]

    def product(left, s, t, groups, g0, g1):
        cells = [(j, g) for j in range(nd * nc) for g in groups]
        tot = None
        for i in range(0, len(cells), 2):
            pair = cells[i:i + 2]
            lhs = jnp.concatenate([left[s, j, g, rows_of(t), :] for j, g in pair], axis=1)
            cols = []
            for n in range(g0, g1):
                los = [(j // m, (j % m) * w + g * LANES) for j, g in pair]
                if len(los) == 2 and los[1] == (los[0][0], los[0][1] + LANES):
                    cols.append(a_col[s, los[0][0], n, los[0][1]:los[0][1] + 2 * LANES, :])
                else:
                    cols.append(jnp.concatenate([a_col[s, b, n, lo:lo + LANES, :] for b, lo in los], axis=0))
            part = jnp.dot(lhs, jnp.concatenate(cols, axis=1), preferred_element_type=jnp.float32)
            tot = part if tot is None else tot + part
        return tot

    def square(s, q):
        g0, g1 = cuts[q]

        @pl.loop(0, h // tm)
        def _(t):
            tot = product(a_row, s, t, range(G), g0, g1) * tile_mask(2 * s + 1, t, g0, g1)
            sq[rows_of(t), g0 * LANES:g1 * LANES] = tot
            v = tot.astype(jnp.bfloat16)
            for g in range(g0, g1):
                s_row[s, me, g, rows_of(t), :] = v[:, (g - g0) * LANES:(g - g0 + 1) * LANES]

    def cubic(s, k, g0, g1):
        cols = slice(g0 * LANES, g1 * LANES)

        @pl.loop(0, h // tm)
        def _(t):
            tot = product(s_row, s, t, range(*cuts[k]), g0, g1)
            if k > 0:
                tot = tot + acc[rows_of(t), cols]
            if k < Q - 1:
                acc[rows_of(t), cols] = tot
                return
            cur = 3.0 * sq[rows_of(t), cols] - 2.0 * (tot * tile_mask(2 * s + 2, t, g0, g1))
            if s < PURIFY - 1:
                v = cur.astype(jnp.bfloat16)
                for g in range(g0, g1):
                    part = v[:, (g - g0) * LANES:(g - g0 + 1) * LANES]
                    a_col[s + 1, r, g, rows_of(t), :] = part
                    a_row[s + 1, me, g, rows_of(t), :] = part
            else:
                out[rows_of(t), cols] = cur

    wide = [(g, min(g + 2, G)) for g in range(0, G, 2)]
    for s in range(PURIFY):
        if s == 0:
            z_own(s, 0, "start")
        ga[s].begin()
        for q in range(Q):
            for dist in range(1, nr):
                z_arrive(s, q, dist)
                if q + 1 < Q and dist == min(2, nr - 1):
                    z_own(s, q + 1, "start")
                if q == 0 and dist == min(2, nr - 1):
                    ga[s].hop()
            if q == 0:
                ga[s].relay()
                ga[s].finish()
            if q >= 2:
                gs[s][q - 2].relay()
            if q >= 1:
                gs[s][q - 1].hop()
            square(s, q)
            gs[s][q].begin()
        if Q >= 2:
            gs[s][Q - 2].relay()
        for k in range(Q):
            if k == max(Q - 2, 0):
                gs[s][Q - 1].hop()
            if k == Q - 1:
                gs[s][k].relay()
            gs[s][k].finish()
            for i, (g0, g1) in enumerate(wide):
                cubic(s, k, g0, g1)
                if k == Q - 1 and s < PURIFY - 1 and g1 == cuts[0][1]:
                    z_own(s + 1, 0, "start")
    for s in range(PURIFY):
        ga[s].drain()
        for q in range(Q):
            z_drain(s, q)
            gs[s][q].drain()


def on_device(dims, density, pattern, filters):
    nd, nr, nc, h, w, tm, cuts = dims
    Q = len(cuts)
    G = w // LANES
    J = nd * nc
    n_peers = J // CORES - 1
    tabs = jnp.concatenate([pattern[None], filters], 0)
    dma = pltpu.SemaphoreType.DMA
    return pl.pallas_call(
        functools.partial(kernel, dims),
        out_shape=jax.ShapeDtypeStruct((h, w), jnp.float32),
        in_specs=[pl.BlockSpec(memory_space=pltpu.VMEM)] * 2,
        out_specs=pl.BlockSpec(memory_space=pltpu.VMEM),
        scratch_shapes=[
            pltpu.VMEM((PURIFY, J, G, h, LANES), jnp.bfloat16),
            pltpu.VMEM((PURIFY, nr, G, h, LANES), jnp.bfloat16),
            pltpu.VMEM((PURIFY, J, G, h, LANES), jnp.bfloat16),
            pltpu.VMEM((h, w), jnp.float32),
            pltpu.VMEM((h, w), jnp.float32),
            pltpu.VMEM((2 * PURIFY + 1, h // tm * 8, w), jnp.float32),
            dma((PURIFY, Q, nr, 2)), dma((PURIFY, Q, nr)),
            dma((PURIFY, n_peers, 2)), dma((PURIFY, n_peers, 2)),
            dma((PURIFY, n_peers + 1)), dma((PURIFY, n_peers + 1)),
            dma((PURIFY, Q, n_peers, 2)), dma((PURIFY, Q, n_peers, 2)),
            dma((PURIFY, Q, n_peers + 1)), dma((PURIFY, Q, n_peers + 1)),
        ],
        compiler_params=pltpu.CompilerParams(
            collective_id=0, has_side_effects=True, vmem_limit_bytes=62 * 2 ** 20),
    )(density, tabs)


def solution(mesh):
    nd, nr, nc = mesh.shape["depth"], mesh.shape["row"], mesh.shape["col"]

    def run(density, pattern, filters):
        h, w = density.shape
        tm = 256 if h % 256 == 0 else h
        groups = w // LANES
        cuts = [(g, g + 1) for g in range(groups)]
        if groups >= 4:
            cuts = [(g, g + 2) for g in range(0, groups - 2, 2)] + cuts[groups - 2:]
        return on_device((nd, nr, nc, h, w, tm, tuple(cuts)), density, pattern, filters)

    return jax.shard_map(
        run,
        mesh=mesh,
        in_specs=(P("row", ("depth", "col")), P(), P()),
        out_specs=P("row", ("depth", "col")),
        check_vma=False,
    )
```

profile of v0, /device:TPU:1, one launch (start us, length us, event | category | flops | bytes accessed | tf_op | source)
XLA Modules:
  0.0 195.9 jit_solution(223184990690256915)
XLA Ops:
  0.0 1.6 pad_add_fusion.tabs
  1.6 191.3 %shard_map.37 = f32[1024,512]{1,0:T(8,128)} custom-call(f32[1024,512]{1,0:T(8,128)} %dens.1, s32[5,64,64]{2,1,0:T(8,128)} %pad_add_fusion.tabs), custom_call_target="tpu_custom_call" | custom-call | tf_op jit(solution)/shard_map/pallas_call | solution.py:319
  192.9 3.1 %copy.5 = f32[1024,512]{1,0:T(8,128)} copy(f32[1024,512]{1,0:T(8,128)} %shard_map.37) | data formatting | bytes 4194304
where the time goes:
time: 196 us
  Pallas kernels  191 us (97%)
  local copies, waits for them, and re-layouts  3.08 us (2%)
    pallas_call x1, Pallas kernels, on_device(): pl.pallas_call(functools.partial(kernel, dims), out_shape=jax.ShapeDtypeS...  191 us

commit v1 on v0

v1 whole, which is shorter than its diff:
```python
import functools

import jax
import jax.numpy as jnp
from jax import lax
from jax.experimental import pallas as pl
from jax.experimental.pallas import tpu as pltpu
from jax.sharding import PartitionSpec as P

BLK = 64
PURIFY = 2
CORES = 2
LANES = 128
MESH = pl.DeviceIdType.MESH


def kernel(dims, dens, pat_in, filt_in, out, a_row, a_col, s_row, sq, acc, mask, pat, filt,
           z_send, z_recv, a_send, a_recv, af_send, af_recv,
           s_send, s_recv, sf_send, sf_recv, o_sem, t_sem):
    nd, nr, nc, h, w, tm, cuts = dims
    Q = len(cuts)
    G = w // LANES
    T = h // tm
    nx = nd // CORES
    m = h // w
    rb, sb = h // BLK, w // BLK
    d, r, c = lax.axis_index("depth"), lax.axis_index("row"), lax.axis_index("col")
    x, core = d // CORES, d % CORES
    sib = x * CORES + (1 - core)
    me = d * nc + c
    peers = [(px, pc) for px in range(nx) for pc in range(nc) if px or pc]
    direct = [p for p, (px, pc) in enumerate(peers) if not (px and pc)]
    bent = [p for p, (px, pc) in enumerate(peers) if px and pc]

    def dev(dd, rr, cc):
        return (dd, rr, cc)

    def peer_to(p):
        px, pc = peers[p]
        return ((x + px) % nx) * CORES + core, (c + pc) % nc

    def peer_from(p, k):
        px, pc = peers[p]
        return ((x + nx - px) % nx) * CORES + k, (c + nc - pc) % nc

    def load(t):
        rows = pl.ds(pl.multiple_of(t * tm, tm), tm)
        return pltpu.make_async_copy(dens.at[rows, :], acc.at[rows, :], o_sem.at[t])

    tables = [pltpu.make_async_copy(pat_in, pat, t_sem.at[0]), pltpu.make_async_copy(filt_in, filt, t_sem.at[1])]
    tables[0].start()
    for t in range(T):
        load(t).start()
    tables[1].start()
    bar = pltpu.get_barrier_semaphore()
    for p in direct:
        dd, cc = peer_to(p)
        pl.semaphore_signal(bar, inc=1, device_id=dev(dd, r, cc), device_id_type=MESH)
    pl.semaphore_signal(bar, inc=1, device_id=dev(sib, r, c), device_id_type=MESH)

    @pl.when(r > 0)
    def _():
        pl.semaphore_signal(bar, inc=1, device_id=dev(d, r - 1, c), device_id_type=MESH)

    @pl.when(r < nr - 1)
    def _():
        pl.semaphore_signal(bar, inc=1, device_id=dev(d, r + 1, c), device_id_type=MESH)

    tb = tm // BLK
    slot = lax.broadcasted_iota(jnp.int32, (T * 8, pat.shape[0]), 0)
    r_pick = (slot // 8 * tb + slot % 8 + r * rb
              == lax.broadcasted_iota(jnp.int32, (T * 8, pat.shape[0]), 1)).astype(jnp.float32)
    c_pick = ((lax.broadcasted_iota(jnp.int32, (pat.shape[1], w), 1) // BLK + me * sb)
              == lax.broadcasted_iota(jnp.int32, (pat.shape[1], w), 0)).astype(jnp.float32)

    def expand(k, table):
        rows = jnp.dot(r_pick, table.astype(jnp.float32), preferred_element_type=jnp.float32)
        mask[k] = jnp.dot(rows, c_pick, preferred_element_type=jnp.float32)

    tables[0].wait()
    expand(0, pat[...])

    def tile_mask(k, t, g0, g1):
        n = (g1 - g0) * LANES
        mk = mask[k, pl.ds(pl.multiple_of(t * 8, 8), 8), g0 * LANES:g1 * LANES][:tb]
        return jnp.broadcast_to(mk[:, None, :], (tb, BLK, n)).reshape(tm, n)

    def rows_of(t):
        return pl.ds(pl.multiple_of(t * tm, tm), tm)

    def operand(t, groups):
        for g in groups:
            v = (acc[rows_of(t), g * LANES:(g + 1) * LANES] * tile_mask(0, t, g, g + 1)).astype(jnp.bfloat16)
            a_col[0, r, g, rows_of(t), :] = v
            a_row[0, me, g, rows_of(t), :] = v

    @pl.loop(0, T)
    def _(t):
        load(t).wait()
        operand(t, range(*cuts[0]))

    near = jnp.minimum(r, 1) + jnp.minimum(nr - 1 - r, 1)
    for n in range(3):
        @pl.when(near == n)
        def _():
            pl.semaphore_wait(bar, len(direct) + 1 + n)

    def z_copy(s, q, src, up):
        ref = a_col.at[s, src, cuts[q][0]:cuts[q][1]]
        return pltpu.make_async_remote_copy(
            src_ref=ref, dst_ref=ref, send_sem=z_send.at[s, q, src, up],
            recv_sem=z_recv.at[s, q, src],
            device_id=dev(d, r + 1 if up else r - 1, c), device_id_type=MESH)

    def z_own(s, q, op):
        @pl.when(r < nr - 1)
        def _():
            getattr(z_copy(s, q, r, 1), op)()

        @pl.when(r > 0)
        def _():
            getattr(z_copy(s, q, r, 0), op)()

    def pass_down(s, q, dist):
        z_copy(s, q, r + dist, 1).wait_recv()
        z_copy(s, q, r + dist, 0).start()

    def pass_up(s, q, dist):
        z_copy(s, q, r - dist, 0).wait_recv()
        z_copy(s, q, r - dist, 1).start()

    def z_fwd(s, q, dist, outer):
        for edge in (0, 1):
            if edge == outer:
                @pl.when((r + dist < nr) & (r > 0) & ((r + dist == nr - 1) == bool(edge)))
                def _():
                    pass_down(s, q, dist)

                @pl.when((r - dist >= 0) & (r < nr - 1) & ((r - dist == 0) == bool(edge)))
                def _():
                    pass_up(s, q, dist)

    def z_inner(s, q):
        for dist in range(1, nr - 1):
            z_fwd(s, q, dist, 0)

    def z_outer(s, q):
        for dist in range(1, nr - 1):
            z_fwd(s, q, dist, 1)

    def z_wait(s, q):
        for dist in range(1, nr):
            @pl.when((r + dist < nr) & (r == 0))
            def _():
                z_copy(s, q, r + dist, 1).wait_recv()

            @pl.when((r - dist >= 0) & (r == nr - 1))
            def _():
                z_copy(s, q, r - dist, 0).wait_recv()

    def z_drain(s, q):
        z_own(s, q, "wait_send")
        for dist in range(1, nr - 1):
            @pl.when((r + dist < nr) & (r > 0))
            def _():
                z_copy(s, q, r + dist, 0).wait_send()

            @pl.when((r - dist >= 0) & (r < nr - 1))
            def _():
                z_copy(s, q, r - dist, 1).wait_send()

    def ac(ref, ss, rs, to):
        return pltpu.make_async_remote_copy(
            src_ref=ref, dst_ref=ref, send_sem=ss, recv_sem=rs,
            device_id=dev(to[0], r, to[1]), device_id_type=MESH)

    class Gather:
        def __init__(self, view, sems, tag):
            self.view, self.sems, self.tag = view, sems, tag

        def sem(self, n, t, *at):
            return self.sems[n].at[(*self.tag, t, *at)]

        def block(self, p, k, t):
            dd, cc = peer_from(p, k)
            return self.view(dd * nc + cc, t * tm, tm)

        def half(self, dd, cc, t, i):
            return self.view(dd * nc + cc, t * tm + i * (tm // 2), tm // 2)

        def path(self, ref, p, t, i, to):
            return ac(ref, self.sem(0, t, p, i), self.sem(1, t, p, i), to)

        def own(self, p, t):
            return self.path(self.view(me, t * tm, tm), p, t, 0, peer_to(p))

        def got(self, p, t, i=None):
            if i is None:
                return self.path(self.block(p, core, t), p, t, 0, peer_to(p))
            dd, cc = peer_from(p, core)
            return self.path(self.half(dd, cc, t, i), p, t, i, peer_to(p))

        def turn(self, p, t, i):
            px, pc = peers[p]
            if i == 0:
                ref = self.half(((x + nx - px) % nx) * CORES + core, c, t, 0)
                to = (d, (c + pc) % nc)
            else:
                ref = self.half(d, (c + nc - pc) % nc, t, 1)
                to = (((x + px) % nx) * CORES + core, c)
            return self.path(ref, p, t, i, to)

        def fwd(self, p, t):
            ref = self.view(me, t * tm, tm) if p == len(peers) else self.block(p, core, t)
            return ac(ref, self.sem(2, t, p), self.sem(3, t, p), (sib, c))

        def fgot(self, p, t):
            ref = self.view(sib * nc + c, t * tm, tm) if p == len(peers) else self.block(p, 1 - core, t)
            return ac(ref, self.sem(2, t, p), self.sem(3, t, p), (sib, c))

        def begin(self, t):
            for p in direct:
                self.own(p, t).start()
            self.fwd(len(peers), t).start()

        def hop(self, t):
            for q in direct:
                self.got(q, t).wait_recv()
                for p in bent:
                    if peers[q] == (peers[p][0], 0):
                        self.turn(p, t, 0).start()
                    if peers[q] == (0, peers[p][1]):
                        self.turn(p, t, 1).start()
            for q in direct:
                self.fwd(q, t).start()

        def relay(self, t):
            for p in bent:
                self.got(p, t, 0).wait_recv()
                self.got(p, t, 1).wait_recv()
                self.fwd(p, t).start()

        def finish(self, t):
            for p in range(len(peers) + 1):
                self.fgot(p, t).wait_recv()

        def drain(self, t):
            for p in direct:
                self.own(p, t).wait_send()
            for p in bent:
                self.turn(p, t, 0).wait_send()
                self.turn(p, t, 1).wait_send()
            for p in range(len(peers) + 1):
                self.fwd(p, t).wait_send()

    def span(lo, n):
        return pl.ds(lo if isinstance(lo, int) else pl.multiple_of(lo, tm // 2), n)

    ga = [Gather(lambda j, lo, n, s=s: a_row.at[s, j, :, span(lo, n)],
                 (a_send, a_recv, af_send, af_recv), (s,)) for s in range(PURIFY)]
    gs = [[Gather(lambda j, lo, n, s=s, q=q: s_row.at[s, j, cuts[q][0]:cuts[q][1], span(lo, n)],
                  (s_send, s_recv, sf_send, sf_recv), (s, q)) for q in range(Q)] for s in range(PURIFY)]

    def product(left, s, t, groups, g0, g1):
        cells = [(j, g) for j in range(nd * nc) for g in groups]
        tot = None
        for i in range(0, len(cells), 2):
            pair = cells[i:i + 2]
            lhs = jnp.concatenate([left[s, j, g, rows_of(t), :] for j, g in pair], axis=1)
            cols = []
            for n in range(g0, g1):
                los = [(j // m, (j % m) * w + g * LANES) for j, g in pair]
                if len(los) == 2 and los[1] == (los[0][0], los[0][1] + LANES):
                    cols.append(a_col[s, los[0][0], n, los[0][1]:los[0][1] + 2 * LANES, :])
                else:
                    cols.append(jnp.concatenate([a_col[s, b, n, lo:lo + LANES, :] for b, lo in los], axis=0))
            part = jnp.dot(lhs, jnp.concatenate(cols, axis=1), preferred_element_type=jnp.float32)
            tot = part if tot is None else tot + part
        return tot

    def square(s, q, t):
        g0, g1 = cuts[q]
        tot = product(a_row, s, t, range(G), g0, g1) * tile_mask(2 * s + 1, t, g0, g1)
        sq[rows_of(t), g0 * LANES:g1 * LANES] = tot
        v = tot.astype(jnp.bfloat16)
        for g in range(g0, g1):
            s_row[s, me, g, rows_of(t), :] = v[:, (g - g0) * LANES:(g - g0 + 1) * LANES]

    def put(t):
        return pltpu.make_async_copy(acc.at[rows_of(t), :], out.at[rows_of(t), :], o_sem.at[t])

    def cubic(s, k, t, g0, g1):
        cols = slice(g0 * LANES, g1 * LANES)
        tot = product(s_row, s, t, range(*cuts[k]), g0, g1)
        if k > 0:
            tot = tot + acc[rows_of(t), cols]
        if k < Q - 1:
            acc[rows_of(t), cols] = tot
            return
        cur = 3.0 * sq[rows_of(t), cols] - 2.0 * (tot * tile_mask(2 * s + 2, t, g0, g1))
        if s < PURIFY - 1:
            v = cur.astype(jnp.bfloat16)
            for g in range(g0, g1):
                part = v[:, (g - g0) * LANES:(g - g0 + 1) * LANES]
                a_col[s + 1, r, g, rows_of(t), :] = part
                a_row[s + 1, me, g, rows_of(t), :] = part
        else:
            acc[rows_of(t), cols] = cur

    wide = [(g, min(g + 2, G)) for g in range(0, G, 2)]
    ready = [[] for _ in range(Q)]
    for k in range(Q - 1):
        for g0, g1 in wide:
            ready[next(q for q in range(k + 1, Q) if q == Q - 1 or cuts[q][1] >= g1)].append((k, (g0, g1)))
    z_own(0, 0, "start")

    @pl.loop(0, T)
    def _(t):
        operand(t, range(cuts[0][1], G))
        ga[0].begin(t)

    tables[1].wait()
    for k in range(filt.shape[0]):
        expand(k + 1, filt[k])
    for s in range(PURIFY):
        ga[s].hop(0)
        z_inner(s, 0)
        if Q > 1:
            z_own(s, 1, "start")
        for t in range(1, T):
            ga[s].hop(t)
        if Q > 1:
            z_inner(s, 1)
        z_outer(s, 0)
        for t in range(T):
            ga[s].relay(t)
        if Q > 1:
            z_outer(s, 1)
        if Q > 2:
            z_own(s, 2, "start")
        z_wait(s, 0)

        @pl.loop(0, T)
        def _(t):
            ga[s].finish(t)
            square(s, 0, t)
            gs[s][0].begin(t)

        for q in range(1, Q):
            if q + 1 < Q:
                z_inner(s, q + 1)
                z_outer(s, q + 1)
                if q + 2 < Q:
                    z_own(s, q + 2, "start")

            @pl.loop(0, T)
            def _(t):
                gs[s][q - 1].hop(t)

            z_wait(s, q)

            @pl.loop(0, T)
            def _(t):
                square(s, q, t)
                gs[s][q].begin(t)

            @pl.loop(0, T)
            def _(t):
                gs[s][q - 1].relay(t)

            @pl.loop(0, T)
            def _(t):
                gs[s][q - 1].finish(t)
                for k, (g0, g1) in ready[q]:
                    cubic(s, k, t, g0, g1)

        @pl.loop(0, T)
        def _(t):
            gs[s][Q - 1].hop(t)

        @pl.loop(0, T)
        def _(t):
            gs[s][Q - 1].relay(t)
            gs[s][Q - 1].finish(t)
            for g0, g1 in wide:
                cubic(s, Q - 1, t, g0, g1)
            if s < PURIFY - 1:
                ga[s + 1].begin(t)
            else:
                put(t).start()

        if s < PURIFY - 1:
            z_own(s + 1, 0, "start")
    for s in range(PURIFY):
        for q in range(Q):
            z_drain(s, q)

        @pl.loop(0, T)
        def _(t):
            ga[s].drain(t)
            for q in range(Q):
                gs[s][q].drain(t)

    @pl.loop(0, T)
    def _(t):
        put(t).wait()


def on_device(dims, density, pattern, filters):
    nd, nr, nc, h, w, tm, cuts = dims
    Q = len(cuts)
    G = w // LANES
    J = nd * nc
    n_peers = J // CORES - 1
    T = h // tm
    dma = pltpu.SemaphoreType.DMA
    return pl.pallas_call(
        functools.partial(kernel, dims),
        out_shape=jax.ShapeDtypeStruct((h, w), jnp.float32),
        in_specs=[pl.BlockSpec(memory_space=pl.ANY)] * 3,
        out_specs=pl.BlockSpec(memory_space=pl.ANY),
        scratch_shapes=[
            pltpu.VMEM((PURIFY, J, G, h, LANES), jnp.bfloat16),
            pltpu.VMEM((PURIFY, nr, G, h, LANES), jnp.bfloat16),
            pltpu.VMEM((PURIFY, J, G, h, LANES), jnp.bfloat16),
            pltpu.VMEM((h, w), jnp.float32),
            pltpu.VMEM((h, w), jnp.float32),
            pltpu.VMEM((2 * PURIFY + 1, T * 8, w), jnp.float32),
            pltpu.VMEM(pattern.shape, jnp.int32), pltpu.VMEM(filters.shape, jnp.int32),
            dma((PURIFY, Q, nr, 2)), dma((PURIFY, Q, nr)),
            dma((PURIFY, T, n_peers, 2)), dma((PURIFY, T, n_peers, 2)),
            dma((PURIFY, T, n_peers + 1)), dma((PURIFY, T, n_peers + 1)),
            dma((PURIFY, Q, T, n_peers, 2)), dma((PURIFY, Q, T, n_peers, 2)),
            dma((PURIFY, Q, T, n_peers + 1)), dma((PURIFY, Q, T, n_peers + 1)),
            dma((T,)), dma((2,)),
        ],
        compiler_params=pltpu.CompilerParams(
            collective_id=0, has_side_effects=True, vmem_limit_bytes=62 * 2 ** 20),
    )(density, pattern, filters)


def solution(mesh):
    nd, nr, nc = mesh.shape["depth"], mesh.shape["row"], mesh.shape["col"]

    def run(density, pattern, filters):
        h, w = density.shape
        tm = 512 if h % 512 == 0 else h
        groups = w // LANES
        cuts = [(g, g + 1) for g in range(groups)]
        if groups >= 4:
            cuts = [(g, g + 2) for g in range(0, groups - 2, 2)] + cuts[groups - 2:]
        return on_device((nd, nr, nc, h, w, tm, tuple(cuts)), density, pattern, filters)

    return jax.shard_map(
        run,
        mesh=mesh,
        in_specs=(P("row", ("depth", "col")), P(), P()),
        out_specs=P("row", ("depth", "col")),
        check_vma=False,
    )
```

time: 196 us -> 182 us (0.929)
  Pallas kernels: 191 us -> 179 us
    pallas_call x1, Pallas kernels: 191 us -> 179 us  [on_device(): pl.pallas_call(functools.partial(kernel, dims), out_shape=jax.ShapeDtypeS...]
where the time goes in v1:
time: 182 us
  Pallas kernels  179 us (98%)
  local copies, waits for them, and re-layouts  3.08 us (2%)
    pallas_call x1, Pallas kernels, on_device(): pl.pallas_call(functools.partial(kernel, dims), out_shape=jax.ShapeDtypeS...  179 us

profile of v1, /device:TPU:1, one launch (start us, length us, event | category | flops | bytes accessed | tf_op | source)
XLA Modules:
  0.0 182.1 jit_solution(11426789204759694072)
XLA Ops:
  0.0 179.0 %shard_map.37 = f32[1024,512]{1,0:T(8,128)} custom-call(f32[1024,512]{1,0:T(8,128)} %dens.1, s32[64,64]{1,0:T(8,128)} %pat_in.1, s32[4,64,64]{2,1,0:T(8,128)} %filt_in.1), custom_call_target="tpu_custom_call" | custom-call | tf_op jit(solution)/shard_map/pallas_call | solution.py:417
  179.0 3.1 %copy.5 = f32[1024,512]{1,0:T(8,128)} copy(f32[1024,512]{1,0:T(8,128)} %shard_map.37) | data formatting | bytes 4194304

commit v2 on v1

--- a/solution.py
+++ b/solution.py
@@ -148,8 +148,8 @@
         for dist in range(1, nr - 1):
             z_fwd(s, q, dist, 1)
 
-    def z_wait(s, q):
-        for dist in range(1, nr):
+    def z_wait(s, q, dists=range(1, nr)):
+        for dist in dists:
             @pl.when((r + dist < nr) & (r == 0))
             def _():
                 z_copy(s, q, r + dist, 1).wait_recv()
@@ -261,8 +261,16 @@
     gs = [[Gather(lambda j, lo, n, s=s, q=q: s_row.at[s, j, cuts[q][0]:cuts[q][1], span(lo, n)],
                   (s_send, s_recv, sf_send, sf_recv), (s, q)) for q in range(Q)] for s in range(PURIFY)]
 
-    def product(left, s, t, groups, g0, g1):
-        cells = [(j, g) for j in range(nd * nc) for g in groups]
+    last = jnp.where(r < nr // 2, nr - 1, 0)
+    early = [i for i in range(nr * m) if i < (nr - 1) * m]
+    late = [i for i in range(nr * m) if i >= (nr - 1) * m]
+
+    def product(left, s, t, groups, g0, g1, part=None):
+        if part is None:
+            cells = [(j, g) for j in range(nd * nc) for g in groups]
+        else:
+            first = lax.rem(last + 1, nr) * m
+            cells = [(lax.rem(first + i, nr * m), g) for i in part for g in groups]
         tot = None
         for i in range(0, len(cells), 2):
             pair = cells[i:i + 2]
@@ -270,17 +278,27 @@
             cols = []
             for n in range(g0, g1):
                 los = [(j // m, (j % m) * w + g * LANES) for j, g in pair]
-                if len(los) == 2 and los[1] == (los[0][0], los[0][1] + LANES):
-                    cols.append(a_col[s, los[0][0], n, los[0][1]:los[0][1] + 2 * LANES, :])
+                if part is not None:
+                    los = [(b, pl.multiple_of(lo, LANES)) for b, lo in los]
+                if len(los) == 2 and (pair[0][0] is pair[1][0] or part is None) and pair[1] == (pair[0][0], pair[0][1] + 1):
+                    cols.append(a_col[s, los[0][0], n, pl.ds(los[0][1], 2 * LANES), :])
                 else:
-                    cols.append(jnp.concatenate([a_col[s, b, n, lo:lo + LANES, :] for b, lo in los], axis=0))
-            part = jnp.dot(lhs, jnp.concatenate(cols, axis=1), preferred_element_type=jnp.float32)
-            tot = part if tot is None else tot + part
+                    cols.append(jnp.concatenate([a_col[s, b, n, pl.ds(lo, LANES), :] for b, lo in los], axis=0))
+            term = jnp.dot(lhs, jnp.concatenate(cols, axis=1), preferred_element_type=jnp.float32)
+            tot = term if tot is None else tot + term
         return tot
 
-    def square(s, q, t):
+    def begun(s, q, t):
         g0, g1 = cuts[q]
-        tot = product(a_row, s, t, range(G), g0, g1) * tile_mask(2 * s + 1, t, g0, g1)
+        sq[rows_of(t), g0 * LANES:g1 * LANES] = product(a_row, s, t, range(G), g0, g1, early)
+
+    def square(s, q, t, split=False):
+        g0, g1 = cuts[q]
+        if split:
+            tot = product(a_row, s, t, range(G), g0, g1, late) + sq[rows_of(t), g0 * LANES:g1 * LANES]
+        else:
+            tot = product(a_row, s, t, range(G), g0, g1)
+        tot = tot * tile_mask(2 * s + 1, t, g0, g1)
         sq[rows_of(t), g0 * LANES:g1 * LANES] = tot
         v = tot.astype(jnp.bfloat16)
         for g in range(g0, g1):
@@ -325,13 +343,15 @@
     for s in range(PURIFY):
         ga[s].hop(0)
         z_inner(s, 0)
-        if Q > 1:
+        if Q > 1 and s > 0:
+            z_own(s, 1, "start")
+        z_outer(s, 0)
+        if Q > 1 and s == 0:
             z_own(s, 1, "start")
         for t in range(1, T):
             ga[s].hop(t)
         if Q > 1:
             z_inner(s, 1)
-        z_outer(s, 0)
         for t in range(T):
             ga[s].relay(t)
         if Q > 1:
@@ -357,11 +377,21 @@
             def _(t):
                 gs[s][q - 1].hop(t)
 
-            z_wait(s, q)
+            split = q == Q - 1
+            if split:
+                z_wait(s, q, range(1, nr - 1))
+
+                @pl.loop(0, T)
+                def _(t):
+                    begun(s, q, t)
+
+                z_wait(s, q, (nr - 1,))
+            else:
+                z_wait(s, q)
 
             @pl.loop(0, T)
             def _(t):
-                square(s, q, t)
+                square(s, q, t, split)
                 gs[s][q].begin(t)
 
             @pl.loop(0, T)

time: 182 us -> 177 us (0.973)
  Pallas kernels: 179 us -> 173 us
    pallas_call x1, Pallas kernels: 179 us -> 173 us  [on_device(): pl.pallas_call(functools.partial(kernel, dims), out_shape=jax.ShapeDtypeS...]
where the time goes in v2:
time: 177 us; the launch traced here: 176 us
  Pallas kernels  173 us (98%)
  local copies, waits for them, and re-layouts  3.08 us (2%)
    pallas_call x1, Pallas kernels, on_device(): pl.pallas_call(functools.partial(kernel, dims), out_shape=jax.ShapeDtypeS...  173 us

profile of v2, /device:TPU:1, one launch (start us, length us, event | category | flops | bytes accessed | tf_op | source)
XLA Modules:
  0.0 176.3 jit_solution(6183010618535766141)
XLA Ops:
  0.0 173.2 %shard_map.37 = f32[1024,512]{1,0:T(8,128)} custom-call(f32[1024,512]{1,0:T(8,128)} %dens.1, s32[64,64]{1,0:T(8,128)} %pat_in.1, s32[4,64,64]{2,1,0:T(8,128)} %filt_in.1), custom_call_target="tpu_custom_call" | custom-call | tf_op jit(solution)/shard_map/pallas_call | solution.py:447
  173.2 3.1 %copy.5 = f32[1024,512]{1,0:T(8,128)} copy(f32[1024,512]{1,0:T(8,128)} %shard_map.37) | data formatting | bytes 4194304

commit v3 on v2

--- a/solution.py
+++ b/solution.py
@@ -16,7 +16,7 @@
 
 def kernel(dims, dens, pat_in, filt_in, out, a_row, a_col, s_row, sq, acc, mask, pat, filt,
            z_send, z_recv, a_send, a_recv, af_send, af_recv,
-           s_send, s_recv, sf_send, sf_recv, o_sem, t_sem):
+           s_send, s_recv, sf_send, sf_recv, o_sem, t_sem, res):
     nd, nr, nc, h, w, tm, cuts = dims
     Q = len(cuts)
     G = w // LANES
@@ -305,7 +305,7 @@
             s_row[s, me, g, rows_of(t), :] = v[:, (g - g0) * LANES:(g - g0 + 1) * LANES]
 
     def put(t):
-        return pltpu.make_async_copy(acc.at[rows_of(t), :], out.at[rows_of(t), :], o_sem.at[t])
+        return pltpu.make_async_copy(res.at[rows_of(t), :], out.at[rows_of(t), :], o_sem.at[t])
 
     def cubic(s, k, t, g0, g1):
         cols = slice(g0 * LANES, g1 * LANES)
@@ -323,7 +323,7 @@
                 a_col[s + 1, r, g, rows_of(t), :] = part
                 a_row[s + 1, me, g, rows_of(t), :] = part
         else:
-            acc[rows_of(t), cols] = cur
+            res[rows_of(t), cols] = cur.astype(jnp.bfloat16)
 
     wide = [(g, min(g + 2, G)) for g in range(0, G, 2)]
     ready = [[] for _ in range(Q)]
@@ -446,7 +446,7 @@
     dma = pltpu.SemaphoreType.DMA
     return pl.pallas_call(
         functools.partial(kernel, dims),
-        out_shape=jax.ShapeDtypeStruct((h, w), jnp.float32),
+        out_shape=jax.ShapeDtypeStruct((h, w), jnp.bfloat16),
         in_specs=[pl.BlockSpec(memory_space=pl.ANY)] * 3,
         out_specs=pl.BlockSpec(memory_space=pl.ANY),
         scratch_shapes=[
@@ -462,11 +462,11 @@
             dma((PURIFY, T, n_peers + 1)), dma((PURIFY, T, n_peers + 1)),
             dma((PURIFY, Q, T, n_peers, 2)), dma((PURIFY, Q, T, n_peers, 2)),
             dma((PURIFY, Q, T, n_peers + 1)), dma((PURIFY, Q, T, n_peers + 1)),
-            dma((T,)), dma((2,)),
+            dma((T,)), dma((2,)), pltpu.VMEM((h, w), jnp.bfloat16),
         ],
         compiler_params=pltpu.CompilerParams(
             collective_id=0, has_side_effects=True, vmem_limit_bytes=62 * 2 ** 20),
-    )(density, pattern, filters)
+    )(density, pattern, filters).astype(jnp.float32)
 
 
 def solution(mesh):

time: 177 us -> 176 us (level)
  local copies, waits for them, and re-layouts: 3.08 us -> 0 us
  other arithmetic: 0 us -> 2.84 us
    unnamed x1 -> x0, local copies, waits for them, and re-layouts: 3.08 us -> none
    convert_element_type x0 -> x1, other arithmetic: none -> 2.84 us  [on_device(): return pl.pallas_call(functools.partial(kernel, dims), out_shape=jax.Shap...]
where the time goes in v3:
time: 176 us
  Pallas kernels  173 us (98%)
  other arithmetic  2.84 us (2%)
    pallas_call x1, Pallas kernels, on_device(): pl.pallas_call(functools.partial(kernel, dims), out_shape=jax.ShapeDtypeS...  173 us

profile of v3, /device:TPU:1, one launch (start us, length us, event | category | flops | bytes accessed | tf_op | source)
XLA Modules:
  0.0 175.9 jit_solution(13059340562317672951)
XLA Ops:
  0.0 173.0 %shard_map.37 = bf16[1024,512]{1,0:T(8,128)(2,1)} custom-call(f32[1024,512]{1,0:T(8,128)} %dens.1, s32[64,64]{1,0:T(8,128)} %pat_in.1, s32[4,64,64]{2,1,0:T(8,128)} %filt_in.1), custom_call_target="tpu_custom_call" | custom-call | tf_op jit(solution)/shard_map/pallas_call | solution.py:447
  173.0 2.8 %convert_element_type.3 = f32[1024,512]{1,0:T(8,128)} convert(bf16[1024,512]{1,0:T(8,128)(2,1)} %shard_map.37) | non-fusion elementwise | flops 524288 | bytes 3145728 | tf_op jit(solution)/shard_map/convert_element_type | solution.py:469
